TPU v7x, 128 devices: a whole 4x4x4 slice. The times are simulated.
128 devices in a mesh: frames: 64 (over z, y, x_lo, core), dp: 2 (over x_hi).
Axes of the slice: x: 4 (x_hi: 2, x_lo: 2; x = x_hi * 2 + x_lo), y: 4, z: 4, core: 2. Of those that a mesh axis runs over, the one named last changes fastest.
Arguments:
- shifted: bfloat16 [2, 256, 16, 16, 640], P('dp', 'frames'), may hold values from -6 to 6
- out_grad: bfloat16 [2, 256, 16, 16, 640], P('dp', 'frames'), may hold values from -6 to 6
- conv_weight: bfloat16 [640, 5760], P('frames'), may hold values from -0.078125 to 0.078125
- norm_gain: float32 [640], replicated, may hold values from 0.5 to 2
- norm_bias: float32 [640], replicated, may hold values from -4 to 4
- shift_fwd: int32 [80], replicated, may hold values from 0 to 639, as said below
- shift_bwd: int32 [80], replicated, may hold values from 0 to 639, as said below
Outputs:
- in_grad: bfloat16 [2, 256, 16, 16, 640], P('dp', 'frames')
- weight_grad: float32 [640, 5760], P('frames')
- gain_grad: float32 [640], replicated
- bias_grad: float32 [640], replicated
Inputs may be any that keep to these rules, and one draw needn't show every extreme that they name: `shift_fwd`: 80 distinct channel numbers, none of them in shift_bwd. `shift_bwd`: 80 distinct channel numbers, none of them in shift_fwd.
All inputs are finite; a program needn't handle non-finite values.
Results may differ from a plain program's by a relative error of at most 0.003.
Values may be sent and summed in bfloat16 or wider, within the bound.
A program may use at most 128 MiB of HBM per device.

v0:
```python
import jax
import jax.numpy as jnp
from jax import lax
from jax.sharding import PartitionSpec as P

GROUP_CH = 20
epsilon = 1e-05


def with_halo(x, sides, width):
    for axis, dim in sides:
        size, length = (lax.axis_size(axis), x.shape[dim])
        up = [(i, (i + 1) % size) for i in range(size - 1)]
        down = [(j, i) for i, j in up]
        last = lax.slice_in_dim(x, length - width, length, axis=dim)
        first = lax.slice_in_dim(x, 0, width, axis=dim)
        before = lax.ppermute(last, axis, up)
        after = lax.ppermute(first, axis, down)
        x = jnp.concatenate([before, x, after], axis=dim)
    return x


def pad_space(values):
    return jnp.pad(values, ((0, 0), (1, 1), (1, 1), (0, 0)))


def on_device(shifted, out_grad, conv_weight, norm_gain, norm_bias, shift_fwd, shift_bwd):
    frames_local = shifted[0]
    grad_local = out_grad[0]
    frame_count, row_count, col_count, channels = frames_local.shape
    groups = channels // GROUP_CH
    whole_weight = lax.all_gather(conv_weight, "frames", axis=0, tiled=True)
    values = frames_local.astype(jnp.float32).reshape(
        frame_count, row_count * col_count, groups, GROUP_CH
    )
    center = jnp.mean(values, axis=(1, 3), keepdims=True)
    spread = jnp.mean(jnp.square(values - center), axis=(1, 3), keepdims=True)
    inverse = lax.rsqrt(spread + epsilon)
    grouped_normed = (values - center) * inverse
    normed = grouped_normed.reshape(frame_count, row_count, col_count, channels)
    before = normed * norm_gain + norm_bias
    activation = jax.nn.silu(before).astype(jnp.bfloat16)
    act_padded = pad_space(activation)
    grad_padded = pad_space(grad_local)
    grad_rows = grad_local.reshape(-1, channels)
    act_grad = jnp.zeros((grad_rows.shape[0], channels), jnp.float32)
    for tap_index in range(9):
        row_off, col_off = divmod(tap_index, 3)
        grad_view = grad_padded[
            :, 2 - row_off : 2 - row_off + row_count, 2 - col_off : 2 - col_off + col_count, :
        ].reshape(-1, channels)
        act_grad = act_grad + jnp.dot(
            grad_view,
            whole_weight[:, tap_index * channels : (tap_index + 1) * channels],
            preferred_element_type=jnp.float32,
        )
    scale = float(
        lax.axis_size("dp") * lax.axis_size("frames") * frame_count * row_count * col_count
    ) ** (-0.5)
    parts = []
    for tap_index in range(9):
        row_off, col_off = divmod(tap_index, 3)
        act_view = act_padded[
            :, row_off : row_off + row_count, col_off : col_off + col_count, :
        ].reshape(-1, channels)
        parts.append(
            lax.dot_general(
                grad_rows, act_view, (((0,), (0,)), ((), ())), preferred_element_type=jnp.float32
            )
        )
    kernel_shard = lax.psum_scatter(
        jnp.concatenate(parts, axis=1), "frames", scatter_dimension=0, tiled=True
    )
    kernel_shard = lax.psum(kernel_shard, "dp")
    weight_grad = kernel_shard * scale
    sigmoid_val = jax.nn.sigmoid(before)
    pre_grad = act_grad.reshape(before.shape) * sigmoid_val * (1.0 + before * (1.0 - sigmoid_val))
    gain_part = jnp.sum(pre_grad * normed, axis=(0, 1, 2))
    bias_part = jnp.sum(pre_grad, axis=(0, 1, 2))
    gain_total, bias_total = lax.psum((gain_part, bias_part), ("frames", "dp"))
    norm_grad = (pre_grad * norm_gain).reshape(values.shape)
    first_mean = jnp.mean(norm_grad, axis=(1, 3), keepdims=True)
    second_mean = jnp.mean(norm_grad * grouped_normed, axis=(1, 3), keepdims=True)
    shifted_grad = (
        ((norm_grad - first_mean - grouped_normed * second_mean) * inverse)
        .reshape(frames_local.shape)
        .astype(jnp.bfloat16)
    )
    channel_ids = jnp.arange(channels, dtype=jnp.int32)
    forward_match = channel_ids[None, :] == shift_fwd[:, None]
    backward_match = channel_ids[None, :] == shift_bwd[:, None]
    forward_select = forward_match.astype(jnp.bfloat16)
    backward_select = backward_match.astype(jnp.bfloat16)
    forward_mask = jnp.any(forward_match, axis=0)
    backward_mask = jnp.any(backward_match, axis=0)
    plane = row_count * col_count
    first_frame = shifted_grad[0].reshape(plane, channels)
    last_frame = shifted_grad[frame_count - 1].reshape(plane, channels)
    contract_channels = (((1,), (1,)), ((), ()))
    rim_first = lax.dot_general(
        forward_select, first_frame, contract_channels, preferred_element_type=jnp.float32
    ).astype(jnp.bfloat16)
    rim_last = lax.dot_general(
        backward_select, last_frame, contract_channels, preferred_element_type=jnp.float32
    ).astype(jnp.bfloat16)
    extended = with_halo(jnp.stack([rim_first, rim_last]), (("frames", 0),), 1)
    contract_fold = (((0,), (0,)), ((), ()))
    from_prev = lax.dot_general(
        extended[0], backward_select, contract_fold, preferred_element_type=jnp.float32
    ).astype(jnp.bfloat16)
    from_next = lax.dot_general(
        extended[3], forward_select, contract_fold, preferred_element_type=jnp.float32
    ).astype(jnp.bfloat16)
    from_prev = from_prev.reshape(1, row_count, col_count, channels)
    from_next = from_next.reshape(1, row_count, col_count, channels)
    later = jnp.concatenate([shifted_grad[1:], from_next], axis=0)
    earlier = jnp.concatenate([from_prev, shifted_grad[:-1]], axis=0)
    in_grad = jnp.where(forward_mask, later, jnp.where(backward_mask, earlier, shifted_grad))
    return (in_grad[None], weight_grad, gain_total * scale, bias_total * scale)


def solution(mesh):
    in_specs = (
        P("dp", "frames", None, None, None),
        P("dp", "frames", None, None, None),
        P("frames", None),
        P(),
        P(),
        P(),
        P(),
    )
    out_specs = (P("dp", "frames", None, None, None), P("frames", None), P(), P())
    return jax.shard_map(
        on_device, mesh=mesh, in_specs=in_specs, out_specs=out_specs, check_vma=False
    )
```

profile of v0, /device:TPU:1, one launch (start us, length us, event | category | flops | bytes accessed | tf_op | source)
XLA Modules:
  0.0 923.6 jit_solution(15676079137542957894)
XLA Ops:
  7.2 0.7 all-gather.3.cloned.1.call-update
  8.0 21.9 %reshape.226 = f32[4,256,32,20]{3,2,1,0:T(8,128)} reshape(bf16[1,4,16,16,640]{4,3,2,1,0:T(8,128)(2,1)} %param.7) | data formatting | bytes 3932160 | tf_op jit(solution)/shard_map/convert_element_type | solution.py:33
  30.6 0.4 multiply_reduce_fusion.2
  31.5 11.5 %copy.33 = f32[4,256,32,20]{1,0,3,2:T(4,128)} copy(f32[4,256,32,20]{3,2,1,0:T(8,128)} %reshape.226) | data formatting | bytes 5242880 | tf_op jit(solution)/shard_map/convert_element_type | solution.py:33
  43.2 8.8 pad_slice_fusion.8
  52.0 78.7 %all-gather.3.cloned.1.call-done = bf16[64,10,5760]{2,1,0:T(8,128)(2,1)} async-done(((bf16[1,10,5760]{2,1,0:T(8,128)(2,1)}), bf16[64,10,5760]{2,1,0:T(8,128)(2,1)}) %all-gather.3.cloned.1.call-update) | async-done | bytes 7372816 | tf_op jit(solution)/shard_map/all_gather | solution.py:32
  130.7 13.8 %reshape.229 = bf16[640,5760]{1,0:T(8,128)(2,1)} reshape(bf16[64,10,5760]{2,1,0:T(8,128)(2,1)} %all-gather.3.cloned.1.call-done) | data formatting | bytes 14745600
  144.6 3.0 fusion.4
  147.6 0.7 copy-done.1
  148.3 0.3 copy-done.11
  148.6 1.3 fusion.6
  149.9 1.3 fusion.8
  151.3 1.3 fusion.10
  152.6 1.3 fusion.12
  154.0 1.3 fusion.14
  155.3 2.8 fusion.18
  158.1 2.8 fusion.16
  160.9 6.2 fusion.28
  167.1 3.3 copy.31
  170.3 4.2 reshape.215
  174.5 16.5 %fusion.29 = (f32[4,32]{0,1:T(8,128)S(1)}, f32[4,32]{0,1:T(8,128)S(1)}) fusion(f32[4,32]{0,1:T(8,128)S(1)} %copy.34, f32[4,256,32,20]{1,0,3,2:T(4,128)} %copy.33, f32[4,32]{0,1:T(8,128)S(1)} %copy.32, f32[4,256,32,20]{1,0,3,2:T(4,128)} %reshape.215, f32[32,20]{1,0:T(8,128)S(1)} %add.134, f32[32,20]{1,0:T(8,128)S(1)} %mul.201), kind=kLoop, calls=%fused_computation.88 | loop fusion | flops 10485504 | bytes 5250048 | tf_op jit(solution)/shard_map/reduce_sum | solution.py:82
  191.6 3.6 multiply_convert_fusion
  195.2 3.0 pad_slice_fusion
  198.2 2.4 bitcast_dynamic-update-slice_fusion.8
  200.6 2.4 bitcast_dynamic-update-slice_fusion.7
  203.0 2.4 bitcast_dynamic-update-slice_fusion.6
  205.5 2.4 bitcast_dynamic-update-slice_fusion.5
  207.9 2.4 bitcast_dynamic-update-slice_fusion.4
  210.3 2.4 bitcast_dynamic-update-slice_fusion.3
  212.7 2.5 bitcast_dynamic-update-slice_fusion.2
  215.2 2.4 bitcast_dynamic-update-slice_fusion.1
  217.6 2.4 bitcast_dynamic-update-slice_fusion
  220.1 0.6 copy-done.16
  220.7 0.6 dynamic-slice
  222.4 2.2 collective-permute-start
  224.9 3.4 collective-permute-start.1
  228.2 67.9 %all-reduce.3 = (f32[640]{0:T(1024)S(1)}, f32[640]{0:T(1024)S(1)}) all-reduce(f32[640]{0:T(1024)S(1)} %get-tuple-element.25, f32[640]{0:T(1024)S(1)} %get-tuple-element.24), channel_id=1, replica_groups=mesh['frames'=64,'dp'=2] {'frames','dp'}, use_global_device_ids=true, to_apply=%region_11.12 | all-reduce | flops 1280 | bytes 10240 | tf_op jit(solution)/shard_map/psum | solution.py:80
  296.1 1.5 slice_bitcast_fusion
  297.6 0.6 broadcast_multiply_fusion.1
  298.2 1.0 convolution_convert_fusion.1
  299.2 1.0 convolution_convert_fusion
  300.3 516.5 %all-reduce.9.cloned.1.call-done = f32[640,5760]{0,1:T(8,128)} async-done(((f32[640,5760]{0,1:T(8,128)}), f32[640,5760]{0,1:T(8,128)}) %all-reduce.9.cloned.1.call-update) | async-done | bytes 14745616
  816.7 5.1 constant_dynamic-slice_fusion
  821.8 1.2 copy-done.2
  823.3 4.4 maximum_select_fusion
  827.7 82.4 %all-reduce.7.cloned.1.call-done = f32[10,5760]{0,1:T(8,128)} async-done(((f32[10,5760]{0,1:T(8,128)}), f32[10,5760]{0,1:T(8,128)}) %all-reduce.7.cloned.1.call-update) | async-done | bytes 230416 | tf_op jit(solution)/shard_map/psum | solution.py:74
  910.1 3.7 broadcast_multiply_fusion
  913.8 3.0 copy.37
  (64 shorter events, 3.1 us)
Async XLA Ops:
  7.2 123.5 %all-gather.3.cloned.1.call-start = ((), (), s32[]{:S(2)}) async-start(), calls=%async_computation.1 | async-start | bytes 11980800 | tf_op jit(solution)/shard_map/all_gather | solution.py:32
  7.9 22.0 %copy-start = (bf16[1,4,16,16,640]{4,3,2,1,0:T(8,128)(2,1)S(1)}, bf16[1,4,16,16,640]{4,3,2,1,0:T(8,128)(2,1)}, u32[]{:S(2)}) copy-start(bf16[1,4,16,16,640]{4,3,2,1,0:T(8,128)(2,1)} %param.7) | copy-start | bytes 3932164
  7.9 808.8 %all-reduce.9.cloned.1.call-start = ((), (), s32[]{:S(2)}) async-start(), calls=%async_computation.2 | async-start | bytes 29491200
  31.5 11.5 %copy-start.12 = (f32[640]{0:T(1024)S(1)}, f32[640]{0:T(1024)}, u32[]{:S(2)}) copy-start(f32[640]{0:T(1024)} %param.11) | copy-start | bytes 7684
  31.5 11.6 %copy-start.13 = (f32[640]{0:T(1024)S(1)}, f32[640]{0:T(1024)}, u32[]{:S(2)}) copy-start(f32[640]{0:T(1024)} %param.10) | copy-start | bytes 7684
  144.5 3.7 copy-start.1
  144.6 4.0 copy-start.11
  148.6 1.3 copy-start.10
  149.9 1.3 copy-start.4
  151.3 1.3 copy-start.9
  152.6 1.3 copy-start.8
  154.0 1.3 copy-start.7
  155.3 2.8 copy-start.6
  195.2 3.0 copy-start.5
  220.1 0.7 copy-start.16
  220.1 1.9 copy-start.14
  220.1 1.9 copy-start.15
  220.1 690.0 %all-reduce.7.cloned.1.call-start = ((), (), s32[]{:S(2)}) async-start(), calls=%async_computation | async-start | bytes 5898240 | tf_op jit(solution)/shard_map/psum | solution.py:74
  222.4 75.8 %collective-permute-start = (bf16[1,80,256]{2,1,0:T(8,128)(2,1)S(1)}, bf16[1,80,256]{2,1,0:T(8,128)(2,1)S(1)}, u32[]{:S(2)}, u32[]{:S(2)}) collective-permute-start(bf16[1,80,256]{2,1,0:T(8,128)(2,1)S(1)} %fusion.1), channel_id=1, source_target_pairs={{2,0},{4,2},{6,4},{8,6},{10,8},{12,10},{14,12},{16,14},{18,16},{20... | collective-permute-start | bytes 122888 | tf_op jit(solution)/shard_map/ppermute | solution.py:18
  224.9 74.4 %collective-permute-start.1 = (bf16[1,80,256]{2,1,0:T(8,128)(2,1)S(1)}, bf16[1,80,256]{2,1,0:T(8,128)(2,1)S(1)}, u32[]{:S(2)}, u32[]{:S(2)}) collective-permute-start(bf16[1,80,256]{2,1,0:T(8,128)(2,1)S(1)} %fusion.2), channel_id=1, source_target_pairs={{0,2},{2,4},{4,6},{6,8},{8,10},{10,12},{12,14},{14,16},{16,18},{18... | collective-permute-start | bytes 122888 | tf_op jit(solution)/shard_map/ppermute | solution.py:17
  821.8 1.2 copy-start.2
  821.8 1.5 copy-start.3
Sparse Core Ops, SparseCore 0:
  9.7 120.9 all-gather.2
  220.2 596.4 all-reduce.8
  822.0 88.0 all-reduce.6
where the time goes:
time: 929 us; the launch traced here: 924 us
  waiting for transfers between devices  678 us (73%)
  local copies, waits for them, and re-layouts  81.4 us (9%)
  blocking collectives  67.9 us (7%)
  matrix products  45.7 us (5%)
  other arithmetic  29.7 us (3%)
  between operations  15 us (2%)
    unnamed x4, waiting for transfers between devices  517 us
    psum x1, waiting for transfers between devices, on_device(): kernel_shard = lax.psum(kernel_shard, 'dp')  82.4 us
    all_gather x1, waiting for transfers between devices, on_device(): whole_weight = lax.all_gather(conv_weight, 'frames', axis=0, tiled=True)  78.7 us
    psum x1, blocking collectives, on_device(): gain_total, bias_total = lax.psum((gain_part, bias_part), ('frames', 'dp'))  67.9 us
    convert_element_type x2, local copies, waits for them, and re-layouts, on_device(): frames_local.astype(jnp.float32)  33.4 us
    unnamed x38, local copies, waits for them, and re-layouts  25.6 us
    dot_general x9, matrix products, on_device(): lax.dot_general(grad_rows, act_view, (((0,), (0,)), ((), ())), preferred_...  21.8 us
    dot_general x9, matrix products, on_device(): jnp.dot(grad_view, whole_weight[:, tap_index * channels:(tap_index + 1) *...  21.3 us
  transfers between devices with their start and end apart: 5, of which 3 were waited for; matrix products, arithmetic and copies ran while one was open for 6% of the time, Pallas kernels for 0%

commit v1 on v0

--- a/solution.py
+++ b/solution.py
@@ -77,7 +77,7 @@
     pre_grad = act_grad.reshape(before.shape) * sigmoid_val * (1.0 + before * (1.0 - sigmoid_val))
     gain_part = jnp.sum(pre_grad * normed, axis=(0, 1, 2))
     bias_part = jnp.sum(pre_grad, axis=(0, 1, 2))
-    gain_total, bias_total = lax.psum((gain_part, bias_part), ("frames", "dp"))
+    gain_total, bias_total = lax.psum(lax.psum((gain_part, bias_part), "frames"), "dp")
     norm_grad = (pre_grad * norm_gain).reshape(values.shape)
     first_mean = jnp.mean(norm_grad, axis=(1, 3), keepdims=True)
     second_mean = jnp.mean(norm_grad * grouped_normed, axis=(1, 3), keepdims=True)

time: 929 us -> 914 us (0.984)
  blocking collectives: 67.9 us -> 145 us
  waiting for transfers between devices: 678 us -> 602 us
  other arithmetic: 29.7 us -> 18.9 us
    psum x1 -> x2, blocking collectives: 67.9 us -> 145 us  [the longest x1 139 us: on_device(): lax.psum((gain_part, bias_part), 'frames')]
    unnamed x4, waiting for transfers between devices: 517 us -> 441 us
    reduce_sum x1, other arithmetic: 16.5 us -> 5.68 us  [on_device(): first_mean = jnp.mean(norm_grad, axis=(1, 3), keepdims=True)]
where the time goes in v1:
time: 914 us; the launch traced here: 913 us
  waiting for transfers between devices  602 us (66%)
  blocking collectives  145 us (16%)
  local copies, waits for them, and re-layouts  81 us (9%)
  matrix products  45.7 us (5%)
  other arithmetic  18.9 us (2%)
  between operations  14.7 us (2%)
    unnamed x4, waiting for transfers between devices  441 us
    psum x1, blocking collectives, on_device(): lax.psum((gain_part, bias_part), 'frames')  139 us
    psum x1, waiting for transfers between devices, on_device(): kernel_shard = lax.psum(kernel_shard, 'dp')  82.4 us
    all_gather x1, waiting for transfers between devices, on_device(): whole_weight = lax.all_gather(conv_weight, 'frames', axis=0, tiled=True)  78.7 us
    convert_element_type x2, local copies, waits for them, and re-layouts, on_device(): frames_local.astype(jnp.float32)  33.4 us
    unnamed x38, local copies, waits for them, and re-layouts  25.3 us
    dot_general x9, matrix products, on_device(): lax.dot_general(grad_rows, act_view, (((0,), (0,)), ((), ())), preferred_...  21.8 us
    dot_general x9, matrix products, on_device(): jnp.dot(grad_view, whole_weight[:, tap_index * channels:(tap_index + 1) *...  21.3 us
  transfers between devices with their start and end apart: 5, of which 3 were waited for; matrix products, arithmetic and copies ran while one was open for 6% of the time, Pallas kernels for 0%

profile of v1, /device:TPU:1, one launch (start us, length us, event | category | flops | bytes accessed | tf_op | source)
XLA Modules:
  0.0 912.8 jit_solution(3813310240220658900)
XLA Ops:
  7.2 0.7 all-gather.3.cloned.1.call-update
  8.0 21.9 %reshape.226 = f32[4,256,32,20]{3,2,1,0:T(8,128)} reshape(bf16[1,4,16,16,640]{4,3,2,1,0:T(8,128)(2,1)} %param.7) | data formatting | bytes 3932160 | tf_op jit(solution)/shard_map/convert_element_type | solution.py:33
  30.6 0.4 multiply_reduce_fusion.2
  31.5 11.5 %copy.33 = f32[4,256,32,20]{1,0,3,2:T(4,128)} copy(f32[4,256,32,20]{3,2,1,0:T(8,128)} %reshape.226) | data formatting | bytes 5242880 | tf_op jit(solution)/shard_map/convert_element_type | solution.py:33
  43.2 8.8 pad_slice_fusion.8
  52.0 78.7 %all-gather.3.cloned.1.call-done = bf16[64,10,5760]{2,1,0:T(8,128)(2,1)} async-done(((bf16[1,10,5760]{2,1,0:T(8,128)(2,1)}), bf16[64,10,5760]{2,1,0:T(8,128)(2,1)}) %all-gather.3.cloned.1.call-update) | async-done | bytes 7372816 | tf_op jit(solution)/shard_map/all_gather | solution.py:32
  130.7 13.5 %reshape.229 = bf16[640,5760]{1,0:T(8,128)(2,1)} reshape(bf16[64,10,5760]{2,1,0:T(8,128)(2,1)} %all-gather.3.cloned.1.call-done) | data formatting | bytes 14745600
  144.2 3.0 fusion.4
  147.2 0.7 copy-done.1
  148.2 1.3 fusion.6
  149.6 1.3 fusion.8
  150.9 1.3 fusion.10
  152.3 1.3 fusion.12
  153.6 1.3 fusion.14
  155.0 2.8 fusion.18
  157.7 2.8 fusion.16
  160.6 6.2 fusion.28
  166.7 3.3 copy.31
  170.0 4.2 reshape.215
  174.2 5.7 fusion.29
  180.4 3.6 multiply_convert_fusion
  184.0 3.0 pad_slice_fusion
  187.0 2.4 bitcast_dynamic-update-slice_fusion.8
  189.4 2.4 bitcast_dynamic-update-slice_fusion.7
  191.9 2.4 bitcast_dynamic-update-slice_fusion.6
  194.3 2.4 bitcast_dynamic-update-slice_fusion.5
  196.7 2.4 bitcast_dynamic-update-slice_fusion.4
  199.1 2.4 bitcast_dynamic-update-slice_fusion.3
  201.5 2.5 bitcast_dynamic-update-slice_fusion.2
  204.0 2.4 bitcast_dynamic-update-slice_fusion.1
  206.5 2.4 bitcast_dynamic-update-slice_fusion
  209.0 0.6 copy-done.16
  209.5 0.6 dynamic-slice
  211.2 2.2 collective-permute-start
  213.7 3.4 collective-permute-start.1
  217.1 139.3 %all-reduce.3 = (f32[640]{0:T(1024)S(1)}, f32[640]{0:T(1024)S(1)}) all-reduce(f32[640]{0:T(1024)S(1)} %get-tuple-element.25, f32[640]{0:T(1024)S(1)} %get-tuple-element.24), channel_id=1, replica_groups=mesh['frames'=64,'dp'=2] {'frames'}, use_global_device_ids=true, to_apply=%region_11.12 | all-reduce | flops 1280 | bytes 10240 | tf_op jit(solution)/shard_map/psum | solution.py:80
  356.4 5.8 all-reduce.4
  362.1 1.5 slice_bitcast_fusion
  363.6 0.6 broadcast_multiply_fusion.1
  364.2 1.0 convolution_convert_fusion.1
  365.3 1.0 convolution_convert_fusion
  366.3 440.0 %all-reduce.10.cloned.1.call-done = f32[640,5760]{0,1:T(8,128)} async-done(((f32[640,5760]{0,1:T(8,128)}), f32[640,5760]{0,1:T(8,128)}) %all-reduce.10.cloned.1.call-update) | async-done | bytes 14745616
  806.3 5.1 constant_dynamic-slice_fusion
  811.3 1.2 copy-done.2
  812.8 4.4 maximum_select_fusion
  817.2 82.4 %all-reduce.8.cloned.1.call-done = f32[10,5760]{0,1:T(8,128)} async-done(((f32[10,5760]{0,1:T(8,128)}), f32[10,5760]{0,1:T(8,128)}) %all-reduce.8.cloned.1.call-update) | async-done | bytes 230416 | tf_op jit(solution)/shard_map/psum | solution.py:74
  899.6 3.7 broadcast_multiply_fusion
  903.3 3.0 copy.37
  (65 shorter events, 3.4 us)
Async XLA Ops:
  7.2 123.5 %all-gather.3.cloned.1.call-start = ((), (), s32[]{:S(2)}) async-start(), calls=%async_computation.1 | async-start | bytes 11980800 | tf_op jit(solution)/shard_map/all_gather | solution.py:32
  7.9 22.0 %copy-start = (bf16[1,4,16,16,640]{4,3,2,1,0:T(8,128)(2,1)S(1)}, bf16[1,4,16,16,640]{4,3,2,1,0:T(8,128)(2,1)}, u32[]{:S(2)}) copy-start(bf16[1,4,16,16,640]{4,3,2,1,0:T(8,128)(2,1)} %param.7) | copy-start | bytes 3932164
  7.9 798.3 %all-reduce.10.cloned.1.call-start = ((), (), s32[]{:S(2)}) async-start(), calls=%async_computation.2 | async-start | bytes 29491200
  31.5 11.5 %copy-start.12 = (f32[640]{0:T(1024)S(1)}, f32[640]{0:T(1024)}, u32[]{:S(2)}) copy-start(f32[640]{0:T(1024)} %param.11) | copy-start | bytes 7684
  31.5 11.6 %copy-start.13 = (f32[640]{0:T(1024)S(1)}, f32[640]{0:T(1024)}, u32[]{:S(2)}) copy-start(f32[640]{0:T(1024)} %param.10) | copy-start | bytes 7684
  144.2 3.7 copy-start.1
  144.2 4.1 copy-start.11
  148.2 1.3 copy-start.10
  149.6 1.3 copy-start.4
  150.9 1.3 copy-start.9
  152.3 1.3 copy-start.8
  153.6 1.3 copy-start.7
  154.9 2.8 copy-start.6
  184.0 3.0 copy-start.5
  208.9 0.7 copy-start.16
  208.9 1.9 copy-start.14
  208.9 1.9 copy-start.15
  208.9 690.7 %all-reduce.8.cloned.1.call-start = ((), (), s32[]{:S(2)}) async-start(), calls=%async_computation | async-start | bytes 5898240 | tf_op jit(solution)/shard_map/psum | solution.py:74
  211.2 153.0 %collective-permute-start = (bf16[1,80,256]{2,1,0:T(8,128)(2,1)S(1)}, bf16[1,80,256]{2,1,0:T(8,128)(2,1)S(1)}, u32[]{:S(2)}, u32[]{:S(2)}) collective-permute-start(bf16[1,80,256]{2,1,0:T(8,128)(2,1)S(1)} %fusion.1), channel_id=1, source_target_pairs={{2,0},{4,2},{6,4},{8,6},{10,8},{12,10},{14,12},{16,14},{18,16},{20... | collective-permute-start | bytes 122888 | tf_op jit(solution)/shard_map/ppermute | solution.py:18
  213.7 151.6 %collective-permute-start.1 = (bf16[1,80,256]{2,1,0:T(8,128)(2,1)S(1)}, bf16[1,80,256]{2,1,0:T(8,128)(2,1)S(1)}, u32[]{:S(2)}, u32[]{:S(2)}) collective-permute-start(bf16[1,80,256]{2,1,0:T(8,128)(2,1)S(1)} %fusion.2), channel_id=1, source_target_pairs={{0,2},{2,4},{4,6},{6,8},{8,10},{10,12},{12,14},{14,16},{16,18},{18... | collective-permute-start | bytes 122888 | tf_op jit(solution)/shard_map/ppermute | solution.py:17
  811.3 1.2 copy-start.2
  811.3 1.5 copy-start.3
Sparse Core Ops, SparseCore 0:
  9.7 120.9 all-gather.2
  209.0 597.1 all-reduce.9
  811.5 88.0 all-reduce.7
